TPU v7x, 32 devices: a whole 2x2x4 slice. The times are simulated.
32 devices in a mesh: dom: 4 (over z), ml: 8 (over y, x, core).
Axes of the slice: x: 2, y: 2, z: 4, core: 2. Of those that a mesh axis runs over, the one named last changes fastest.
Arguments:
- mm_positions: float32 [3, 65536], P(None, ('dom', 'ml')), may hold values from -6 to 6
- mm_charge: float32 [65536], P(('dom', 'ml')), may hold values from -1 to 1
- mm_tiles: int32 [512, 8], P(('dom', 'ml')), may hold values from 0 to 47, as said below
- ml_feat: bfloat16 [32, 512, 128], P('dom', 'ml'), may hold values from -6 to 6
- ml_positions: float32 [32, 3, 512], P('dom', None, 'ml'), may hold values from -6 to 6
- ml_neighbours: int32 [32, 32, 512], P('dom', None, 'ml'), may hold values from 0 to 511
- msg_weight: bfloat16 [2, 128, 128], replicated, may hold values from -0.5 to 0.5
- radial_weight: float32 [2, 8, 128], replicated, may hold values from -5 to 5
- out_weight: bfloat16 [2, 128, 128], replicated, may hold values from -0.5 to 0.5
- read_weight: bfloat16 [128, 256], replicated, may hold values from -0.5 to 0.5
Outputs:
- mm_force: float32 [3, 65536], P(None, ('dom', 'ml'))
- ml_force: float32 [32, 3, 512], P('dom', None, 'ml')
Inputs may be any that keep to these rules, and one draw needn't show every extreme that they name: `mm_tiles`: for each tile of a device, 8 distinct positions among the 16 tiles of the previous device along dom+ml (wrapping), its own tiles and the next device's, in that order; at least one lies among the previous device's tiles and at least one among the next device's. `ml_neighbours`: indices of atoms within the same patch.
All inputs are finite; a program needn't handle non-finite values.
Results may differ from a plain program's by a relative error of at most 0.007.
Values may be sent and summed in bfloat16 or wider, within the bound.
A program may use at most 320 MiB of HBM per device.

v0:
```python
import functools
import math

import jax
import jax.numpy as jnp
from jax import lax
from jax.experimental import pallas as pl
from jax.experimental.pallas import tpu as pltpu
from jax.sharding import PartitionSpec as P

TILE = 128
RADIUS = 6.0
SOFTEN = 1.0
COULOMB = 0.5
CHUNK = 64
WAVE = (0.261799388, -0.00299057413, 1.02484123e-05, -1.67106067e-08, 1.52995984e-11)
F32 = jnp.float32
BF16 = jnp.bfloat16
MESH = pl.DeviceIdType.MESH
ANY = pl.BlockSpec(memory_space=pl.ANY)
VMEM = pl.BlockSpec(memory_space=pltpu.VMEM)


def split3(x):
    high = x.astype(BF16).astype(F32)
    rest = x - high
    middle = rest.astype(BF16).astype(F32)
    return high, middle, (rest - middle).astype(BF16).astype(F32)


def last_row(shape):
    return lax.broadcasted_iota(jnp.int32, shape, 0) == 3


def left_factor(xyz):
    norm = jnp.sum(xyz * xyz, axis=0, keepdims=True)
    high, middle, low = split3(jnp.concatenate([xyz, norm], axis=0))
    last = last_row(high.shape)
    one = jnp.ones_like(high)
    groups = [
        high,
        jnp.where(last, middle, high),
        jnp.where(last, low, middle),
        jnp.where(last, one, high),
        jnp.where(last, one, low),
        jnp.where(last, one, middle),
        jnp.zeros_like(high),
        jnp.zeros_like(high),
    ]
    return jnp.concatenate(groups, axis=0)


def right_factor(xyz):
    norm = jnp.sum(xyz * xyz, axis=0, keepdims=True) + SOFTEN
    high, middle, low = split3(jnp.concatenate([-2.0 * xyz, norm], axis=0))
    last = last_row(high.shape)
    one = jnp.ones_like(high)
    groups = [
        jnp.where(last, one, high),
        jnp.where(last, one, middle),
        jnp.where(last, one, high),
        low,
        high,
        middle,
        jnp.zeros_like(high),
        jnp.zeros_like(high),
    ]
    return jnp.concatenate(groups, axis=0).astype(BF16)


def moment_rows(xyz, weight):
    rows = jnp.concatenate([xyz * weight, weight], axis=0)
    high, middle, low = split3(rows)
    return jnp.concatenate([high, middle, low, jnp.zeros_like(high)], axis=0).astype(BF16)


def folded(moments):
    return moments[0:4] + moments[4:8] + moments[8:12]


def dot(a, b):
    return jnp.dot(a, b, preferred_element_type=F32)


def half_wave(w):
    y = w * w
    p = WAVE[-1]
    for c in WAVE[-2::-1]:
        p = p * y + c
    return p * w


def kernel(
    shape,
    mm_pos,
    mm_charge,
    mm_tiles,
    feat,
    pos,
    nbr,
    msg_w,
    rad_w,
    out_w,
    read_w,
    mm_out,
    ml_out,
    win_p,
    win_q,
    tiles,
    feat_buf,
    nbr_own,
    pos_own,
    geo_own,
    geo_buf,
    msg_v,
    rad_v,
    out_v,
    read_v,
    turned,
    read_t,
    near_v,
    near_r,
    own_u,
    word_s,
    value_s,
    count_s,
    basis,
    spread,
    weight_s,
    rad_cols,
    stage,
    force_buf,
    local_sem,
    halo_send,
    halo_recv,
    ml_send,
    ml_recv,
    back_send,
    back_recv,
    all_in,
):
    doms, mls = shape
    patches = feat.shape[0]
    atoms = feat.shape[1]
    nbrs = nbr.shape[1]
    psize = mls * atoms
    layers, nb, width = rad_w.shape
    tile_nbrs, tile_count = mm_tiles.shape

    dom = lax.axis_index("dom")
    me = lax.axis_index("ml")
    flat = dom * mls + me
    after = lax.rem(flat + 1, doms * mls)
    before = lax.rem(flat + doms * mls - 1, doms * mls)
    sides = [(before // mls, lax.rem(before, mls)), (after // mls, lax.rem(after, mls))]
    my_patch = lax.rem(me, patches)

    loads = [
        pltpu.make_async_copy(nbr, nbr_own, local_sem.at[7]),
        pltpu.make_async_copy(pos, pos_own, local_sem.at[8]),
    ]
    local = [
        pltpu.make_async_copy(mm_pos, win_p.at[1], local_sem.at[0]),
        pltpu.make_async_copy(mm_charge, win_q.at[1], local_sem.at[1]),
        pltpu.make_async_copy(mm_tiles, tiles, local_sem.at[2]),
        pltpu.make_async_copy(msg_w, msg_v, local_sem.at[3]),
        pltpu.make_async_copy(rad_w, rad_v, local_sem.at[4]),
        pltpu.make_async_copy(out_w, out_v, local_sem.at[5]),
        pltpu.make_async_copy(read_w, read_v, local_sem.at[6]),
        pltpu.make_async_copy(feat.at[my_patch], feat_buf.at[me], local_sem.at[9]),
    ]
    for copy in loads + local:
        copy.start()

    barrier = pltpu.get_barrier_semaphore()
    low, high = me == 0, me == mls - 1
    edge = low | high
    for target in range(1, mls - 1):

        @pl.when(me != target)
        def _():
            pl.semaphore_signal(barrier, inc=1, device_id=(dom, target), device_id_type=MESH)

    for at_edge, side in zip((low, high), sides):

        @pl.when(at_edge)
        def _():
            pl.semaphore_signal(barrier, inc=1, device_id=side, device_id_type=MESH)

    peers = [lax.rem(me + o, mls) for o in range(1, mls)]

    for copy in loads:
        copy.wait()
    quarter = nbrs // 4
    assert nbrs % 4 == 0 and psize & (psize - 1) == 0 and psize <= 4096
    for p in range(patches):
        pairs = nbr_own[p, : 2 * quarter] + psize * nbr_own[p, 2 * quarter :]
        pairs = jnp.concatenate([pairs[:quarter], pairs[quarter:]], axis=1)
        geo_own[p, :quarter] = pairs.astype(F32)
        geo_own[p, quarter : quarter + 3, :atoms] = pos_own[:, p, :]
        geo_own[p, quarter : quarter + 3, atoms:] = pos_own[:, p, :]
        geo_own[p, quarter + 3 :] = jnp.zeros((geo_own.shape[1] - quarter - 3, 2 * atoms), F32)

    @pl.when(jnp.logical_not(edge))
    def _():
        pl.semaphore_wait(barrier, mls - 1)

    for inner, outer in ((1, 0), (mls - 2, mls - 1)):

        @pl.when(me == inner)
        def _():
            pl.semaphore_signal(all_in, inc=1, device_id=(dom, outer), device_id_type=MESH)

    @pl.when(edge)
    def _():
        pl.semaphore_wait(all_in, 1)


    halo = []
    for k, (side, slab) in enumerate(zip(sides, (2, 0))):
        for m, (src, dst) in enumerate(((mm_pos, win_p), (mm_charge, win_q))):
            halo.append(
                pltpu.make_async_remote_copy(
                    src_ref=src,
                    dst_ref=dst.at[slab],
                    send_sem=halo_send.at[2 * k + m],
                    recv_sem=halo_recv.at[2 * k + m],
                    device_id=side,
                    device_id_type=MESH,
                )
            )
    moves = []
    for m, (src, dst) in enumerate(((geo_own, geo_buf), (feat, feat_buf))):
        group = []
        for o, peer in enumerate(peers):
            group.append(
                pltpu.make_async_remote_copy(
                    src_ref=src.at[lax.rem(peer, patches)],
                    dst_ref=dst.at[me],
                    send_sem=ml_send.at[m, o],
                    recv_sem=ml_recv.at[m, o],
                    device_id=(dom, peer),
                    device_id_type=MESH,
                )
            )
        for copy in group:
            copy.start()
        moves.append(group)
    for k, at_edge in enumerate((low, high)):

        @pl.when(jnp.logical_not(at_edge))
        def _():
            for copy in halo[2 * k : 2 * k + 2]:
                copy.start()


    geo_buf[me] = geo_own[my_patch]
    for copy in local:
        copy.wait()
    for l in range(layers):
        turned[l] = msg_v[l].astype(F32).T.astype(BF16)
        turned[layers + l] = out_v[l].astype(F32).T.astype(BF16)
    read_t[...] = read_v[...].astype(F32).T.astype(BF16)
    center = nb // 2
    step = RADIUS / nb
    factors = [
        math.exp(-2.0 * (step * (n - center)) ** 2) / math.sqrt(nbrs) for n in range(nb)
    ]
    for l in range(layers):
        columns = jnp.concatenate([rad_v[l], jnp.zeros((width - nb, width), F32)], axis=0).T
        for n in range(nb):
            rad_cols[l, n] = jnp.broadcast_to(columns[:, n : n + 1] * factors[n], (width, TILE))
    left = left_factor(win_p[1])
    for t in range(tile_count):
        own_u[t] = left[:, t * TILE : (t + 1) * TILE].T.astype(BF16)

    def near_slab(slab):
        xyz = win_p[slab]
        right = right_factor(xyz)
        rows = moment_rows(xyz, win_q[slab])
        for t in range(tile_count):
            near_v[slab * tile_count + t] = right[:, t * TILE : (t + 1) * TILE]
            near_r[slab * tile_count + t] = rows[:, t * TILE : (t + 1) * TILE]

    near_slab(1)

    def mm_tile(t, carry):
        own = own_u[t]
        total = jnp.zeros((16, TILE), F32)
        for c in range(0, tile_nbrs, 2):
            one, two = tiles[c, t], tiles[c + 1, t]
            right = jnp.concatenate([near_v[one], near_v[two]], axis=1)
            rows = jnp.concatenate([near_r[one], near_r[two]], axis=1)
            inverse = lax.rsqrt(dot(own, right))
            cubed = (inverse * inverse * inverse).astype(BF16)
            total = total + lax.dot_general(
                rows, cubed, (((1,), (1,)), ((), ())), preferred_element_type=F32
            )
        at = pl.ds(pl.multiple_of(t * TILE, TILE), TILE)
        sums = folded(total)
        force = win_p[1, :, at] * sums[3:4] - sums[0:3]
        mm_out[:, at] = force * (COULOMB * win_q[1, :, at])
        return carry

    @pl.when(edge)
    def _():
        pl.semaphore_wait(barrier, 1)

    for k, at_edge in enumerate((low, high)):

        @pl.when(at_edge)
        def _():
            for copy in halo[2 * k : 2 * k + 2]:
                copy.start()

    for copy in moves[0]:
        copy.wait_recv()
    pieces = [geo_buf[d] for d in range(mls)]
    pairs = jnp.concatenate(
        [
            jnp.concatenate([piece[:quarter, :atoms] for piece in pieces], axis=1),
            jnp.concatenate([piece[:quarter, atoms:] for piece in pieces], axis=1),
        ],
        axis=0,
    ).astype(jnp.int32)
    bits = psize.bit_length() - 1
    listed = jnp.concatenate([pairs & (psize - 1), jnp.right_shift(pairs, bits)], axis=0)
    words = psize // 4
    half = psize // 8
    word_s[...] = listed & (half - 1)
    value_s[...] = jnp.left_shift(1, 4 * jnp.right_shift(listed, bits - 3))
    xyz = jnp.concatenate([piece[quarter : quarter + 3, :atoms] for piece in pieces], axis=1)
    senders = left_factor(xyz).T.astype(BF16)
    receivers = right_factor(xyz)
    rows = moment_rows(xyz, jnp.ones_like(xyz[0:1]))
    weight_s[...] = dot(senders, receivers)
    for ib in range(psize // TILE):
        at = slice(ib * TILE, (ib + 1) * TILE)
        place = lax.broadcasted_iota(jnp.int32, (words // 2, TILE), 0)
        even = jnp.zeros((words // 2, TILE), jnp.int32)
        odd = even
        for first in range(0, nbrs, 15):
            counts = jnp.zeros((words // 2, TILE), jnp.int32)
            for k in range(first, min(first + 15, nbrs)):
                hit = place == word_s[k : k + 1, at]
                counts = counts + jnp.where(hit, value_s[k : k + 1, at], 0)
            even = even + (counts & 0x0F0F0F0F)
            odd = odd + (jnp.right_shift(counts, 4) & 0x0F0F0F0F)
        count_s[: words // 2] = even
        count_s[words // 2 :] = odd
        for b in range(4):
            for c in range(0, words, CHUNK):
                row = b * words + c
                rows_at = slice(row, row + CHUNK)
                count = (jnp.right_shift(count_s[c : c + CHUNK], 8 * b) & 255).astype(F32)
                squared = weight_s[rows_at, at]
                distance = jnp.minimum(squared * lax.rsqrt(squared), RADIUS)
                wave = half_wave(RADIUS - distance)
                weight = count * (wave * wave)
                weight_s[rows_at, at] = weight
                shifted = distance - center * step
                scaled = shifted * (4.0 * step / math.log(2.0))
                middle = weight * jnp.exp2(shifted * shifted * (-2.0 / math.log(2.0)))
                up = jnp.exp2(scaled)
                down = jnp.exp2(-scaled)
                basis[center * psize + row : center * psize + row + CHUNK, at] = middle.astype(BF16)
                value = middle
                for n in range(center + 1, nb):
                    value = value * up
                    basis[n * psize + row : n * psize + row + CHUNK, at] = value.astype(BF16)
                value = middle
                for n in range(center - 1, -1, -1):
                    value = value * down
                    basis[n * psize + row : n * psize + row + CHUNK, at] = value.astype(BF16)

    for copy in moves[1]:
        copy.wait_recv()
    hidden = feat_buf[...].reshape(psize, width).astype(F32).T.astype(BF16)
    for l in range(layers):
        mixed = dot(turned[l], hidden).astype(BF16)
        wide = mixed.astype(F32)
        for n in range(nb):
            column = jnp.concatenate([rad_cols[l, n]] * (psize // TILE), axis=1)
            spread[:, n * psize : (n + 1) * psize] = (column * wide).astype(BF16)
        message = dot(spread[...], basis[...])
        active = (message / (1.0 + jnp.exp(-message))).astype(BF16)
        update = dot(turned[layers + l], active)
        hidden = (hidden.astype(F32) + update).astype(BF16)
    readout = dot(read_t[...], hidden)
    query = readout[:width].astype(BF16)
    key = readout[width:].T.astype(BF16)
    strength = dot(key, query) * weight_s[...] * (1.0 / width)
    strong = strength.astype(BF16)
    weak = (strength - strong.astype(F32)).astype(BF16)
    sums = folded(dot(rows, strong) + dot(rows, weak))
    force = sums[0:3] - xyz * sums[3:4]
    for d in range(mls):
        stage[d] = force[:, d * atoms : (d + 1) * atoms]
    group = me - my_patch
    returns = []
    for o in range(1, patches):
        owner = group + lax.rem(my_patch + o, patches)
        copy = pltpu.make_async_remote_copy(
            src_ref=stage.at[owner],
            dst_ref=force_buf.at[my_patch],
            send_sem=back_send.at[o - 1],
            recv_sem=back_recv.at[o - 1],
            device_id=(dom, owner),
            device_id_type=MESH,
        )
        copy.start()
        returns.append(copy)
    own = pltpu.make_async_copy(stage.at[me], force_buf.at[my_patch], local_sem.at[0])
    own.start()

    for copy in halo:
        copy.wait_recv()
    near_slab(0)
    near_slab(2)
    lax.fori_loop(0, tile_count, mm_tile, 0, unroll=True)

    for copy in halo:
        copy.wait_send()
    for group in moves:
        for copy in group:
            copy.wait_send()
    own.wait()
    for copy in returns:
        copy.wait()
    for p in range(patches):
        ml_out[:, p, :] = force_buf[p]


def on_device(
    shape,
    mm_positions,
    mm_charge,
    mm_tiles,
    ml_feat,
    ml_positions,
    ml_neighbours,
    msg_weight,
    radial_weight,
    out_weight,
    read_weight,
):
    mls = shape[1]
    patches, atoms, width = ml_feat.shape
    nbrs = ml_neighbours.shape[1]
    psize = mls * atoms
    layers, nb, _ = radial_weight.shape
    count = mm_positions.shape[1]
    tile_count = count // TILE
    dma = pltpu.SemaphoreType.DMA
    geo_rows = (nbrs // 4 + 3 + 7) // 8 * 8
    mm_force, ml_force = pl.pallas_call(
        functools.partial(kernel, shape),
        out_shape=(
            pltpu.VMEM((3, count), F32),
            pltpu.VMEM((3, patches, atoms), F32),
        ),
        in_specs=[ANY] * 10,
        out_specs=(VMEM, VMEM),
        scratch_shapes=[
            pltpu.VMEM((3, 3, count), F32),
            pltpu.VMEM((3, 1, count), F32),
            pltpu.SMEM(mm_tiles.shape[::-1], jnp.int32),
            pltpu.VMEM((mls, atoms, width), BF16),
            pltpu.VMEM((patches, nbrs, atoms), jnp.int32),
            pltpu.VMEM((3, patches, atoms), F32),
            pltpu.VMEM((patches, geo_rows, 2 * atoms), F32),
            pltpu.VMEM((mls, geo_rows, 2 * atoms), F32),
            pltpu.VMEM(msg_weight.shape, BF16),
            pltpu.VMEM(radial_weight.shape, F32),
            pltpu.VMEM(out_weight.shape, BF16),
            pltpu.VMEM(read_weight.shape, BF16),
            pltpu.VMEM((2 * layers, width, width), BF16),
            pltpu.VMEM(read_weight.shape[::-1], BF16),
            pltpu.VMEM((3 * tile_count, 32, TILE), BF16),
            pltpu.VMEM((3 * tile_count, 16, TILE), BF16),
            pltpu.VMEM((tile_count, TILE, 32), BF16),
            pltpu.VMEM((nbrs, psize), jnp.int32),
            pltpu.VMEM((nbrs, psize), jnp.int32),
            pltpu.VMEM((psize // 4, TILE), jnp.int32),
            pltpu.VMEM((nb * psize, psize), BF16),
            pltpu.VMEM((width, nb * psize), BF16),
            pltpu.VMEM((psize, psize), F32),
            pltpu.VMEM((layers, nb, width, TILE), F32),
            pltpu.VMEM((mls, 3, atoms), F32),
            pltpu.VMEM((patches, 3, atoms), F32),
            dma((10,)),
            dma((4,)),
            dma((4,)),
            dma((2, mls)),
            dma((2, mls)),
            dma((patches,)),
            dma((patches,)),
            pltpu.SemaphoreType.REGULAR,
        ],
        compiler_params=pltpu.CompilerParams(
            collective_id=0, has_side_effects=True, vmem_limit_bytes=60 * 1024 * 1024
        ),
        name="force_step",
    )(
        mm_positions,
        mm_charge.reshape(1, count),
        mm_tiles.T,
        ml_feat,
        ml_positions.transpose(1, 0, 2),
        ml_neighbours,
        msg_weight,
        radial_weight,
        out_weight,
        read_weight,
    )
    return mm_force, ml_force.transpose(1, 0, 2)


def solution(mesh):
    shape = (mesh.shape["dom"], mesh.shape["ml"])
    in_specs = (
        P(None, ("dom", "ml")),
        P(("dom", "ml")),
        P(("dom", "ml"), None),
        P("dom", "ml", None),
        P("dom", None, "ml"),
        P("dom", None, "ml"),
        P(),
        P(),
        P(),
        P(),
    )
    out_specs = (P(None, ("dom", "ml")), P("dom", None, "ml"))
    return jax.shard_map(
        functools.partial(on_device, shape),
        mesh=mesh,
        in_specs=in_specs,
        out_specs=out_specs,
        check_vma=False,
    )
```

profile of v0, /device:TPU:0, one launch (start us, length us, event | category | flops | bytes accessed | tf_op | source)
XLA Modules:
  0.0 20.6 jit_solution(17453719166576432186)
XLA Ops:
  0.6 18.8 %force_step.1 = (f32[3,2048]{1,0:T(4,128)S(1)}, f32[3,8,64]{2,1,0:T(8,128)S(1)}) custom-call(f32[3,2048]{1,0:T(4,128)} %mm_pos.1, f32[1,2048]{1,0:T(1,128)} %bitcast.6, s32[8,16]{1,0:T(8,128)} %bitcast.7, bf16[8,64,128]{2,1,0:T(8,128)(2,1)} %feat.1, f32[3,8,64]{2,1,0:T(8,128)} %bitcast.5, s32[8,32,64]{2,1,0:T(8,128)} %nbr.1, bf16[2,128,128]{2,1,0:T(8,128)(2,1)} %msg_w.1, ...), custom_call_target="tpu_custom_call" | custom-call | tf_op jit(solution)/shard_map/force_step/pallas_call | solution.py:456
  19.4 0.6 %copy.14 = f32[3,2048]{1,0:T(4,128)} copy(f32[3,2048]{1,0:T(4,128)S(1)} %get-tuple-element.6) | data formatting | bytes 49152
  20.0 0.6 %copy.15 = f32[8,3,64]{2,0,1:T(8,128)} copy(f32[8,3,64]{2,0,1:T(8,128)S(1)} %bitcast.4) | data formatting | bytes 12288
where the time goes:
time: 20.8 us; the launch traced here: 20.6 us
  Pallas kernels  18.8 us (90%)
  local copies, waits for them, and re-layouts  1.22 us (6%)
  between operations  0.64 us (3%)
    pallas_call x1, Pallas kernels, on_device(): pl.pallas_call(functools.partial(kernel, shape), out_shape=(pltpu.VMEM((3...  18.8 us
    unnamed x2, local copies, waits for them, and re-layouts  1.22 us

commit v1 on v0

--- a/solution.py
+++ b/solution.py
@@ -286,16 +286,19 @@
 
     def mm_tile(t, carry):
         own = own_u[t]
-        total = jnp.zeros((16, TILE), F32)
+        cubes, rows = [], []
         for c in range(0, tile_nbrs, 2):
             one, two = tiles[c, t], tiles[c + 1, t]
             right = jnp.concatenate([near_v[one], near_v[two]], axis=1)
-            rows = jnp.concatenate([near_r[one], near_r[two]], axis=1)
+            rows += [near_r[one], near_r[two]]
             inverse = lax.rsqrt(dot(own, right))
-            cubed = (inverse * inverse * inverse).astype(BF16)
-            total = total + lax.dot_general(
-                rows, cubed, (((1,), (1,)), ((), ())), preferred_element_type=F32
-            )
+            cubes.append((inverse * inverse * inverse).astype(BF16))
+        total = lax.dot_general(
+            jnp.concatenate(cubes, axis=1),
+            jnp.concatenate(rows, axis=1),
+            (((1,), (1,)), ((), ())),
+            preferred_element_type=F32,
+        ).T
         at = pl.ds(pl.multiple_of(t * TILE, TILE), TILE)
         sums = folded(total)
         force = win_p[1, :, at] * sums[3:4] - sums[0:3]

time: 20.8 us -> 18.6 us (0.89)
  Pallas kernels: 18.8 us -> 16.5 us
    pallas_call x1, Pallas kernels: 18.8 us -> 16.5 us  [on_device(): pl.pallas_call(functools.partial(kernel, shape), out_shape=(pltpu.VMEM((3...]
where the time goes in v1:
time: 18.6 us; the launch traced here: 18.4 us
  Pallas kernels  16.5 us (89%)
  local copies, waits for them, and re-layouts  1.22 us (7%)
  between operations  0.64 us (3%)
    pallas_call x1, Pallas kernels, on_device(): pl.pallas_call(functools.partial(kernel, shape), out_shape=(pltpu.VMEM((3...  16.5 us
    unnamed x2, local copies, waits for them, and re-layouts  1.22 us

profile of v1, /device:TPU:0, one launch (start us, length us, event | category | flops | bytes accessed | tf_op | source)
XLA Modules:
  0.0 18.4 jit_solution(15686561586110034547)
XLA Ops:
  0.6 16.5 %force_step.1 = (f32[3,2048]{1,0:T(4,128)S(1)}, f32[3,8,64]{2,1,0:T(8,128)S(1)}) custom-call(f32[3,2048]{1,0:T(4,128)} %mm_pos.1, f32[1,2048]{1,0:T(1,128)} %bitcast.6, s32[8,16]{1,0:T(8,128)} %bitcast.7, bf16[8,64,128]{2,1,0:T(8,128)(2,1)} %feat.1, f32[3,8,64]{2,1,0:T(8,128)} %bitcast.5, s32[8,32,64]{2,1,0:T(8,128)} %nbr.1, bf16[2,128,128]{2,1,0:T(8,128)(2,1)} %msg_w.1, ...), custom_call_target="tpu_custom_call" | custom-call | tf_op jit(solution)/shard_map/force_step/pallas_call | solution.py:459
  17.2 0.6 %copy.14 = f32[3,2048]{1,0:T(4,128)} copy(f32[3,2048]{1,0:T(4,128)S(1)} %get-tuple-element.6) | data formatting | bytes 49152
  17.8 0.6 %copy.15 = f32[8,3,64]{2,0,1:T(8,128)} copy(f32[8,3,64]{2,0,1:T(8,128)S(1)} %bitcast.4) | data formatting | bytes 12288
